TPU v7x, 32 devices: a whole 2x2x4 slice. The times are simulated.
32 devices in a mesh: groups: 2 (over x), tm: 8 (over z, y), state: 2 (over core).
Axes of the slice: x: 2, y: 2, z: 4, core: 2. Of those that a mesh axis runs over, the one named last changes fastest.
Arguments:
- observed: int32 [512], P(('groups', 'tm')), parts along dimension 0, may hold values from 0 to 255
- block_mask: int32 [64, 64], replicated, may hold values 0 or 1
- jump_logit: float32 [512, 512], replicated, may hold values from -4 to 4
- leave_rate: float32 [512], replicated, may hold values from 0.0003 to 0.05
- emit_logit: float32 [256, 512], replicated, may hold values from -3.95 to 4.55
- prior_logit: float32 [512], replicated, may hold values from -4 to 4
Outputs:
- marginals: float32 [512, 512], P(('groups', 'tm'), 'state'), parts along dimension 0
There are 2 independent parts, one for each index of `groups`. A program takes and returns all parts, laid end to end along the dimension named above; an argument that names none is the same for every part. Nothing has to cross between parts.
All inputs are finite; a program needn't handle non-finite values.
Results may differ from a plain program's by a relative error of at most 0.0003.
Values sent between devices are 32-bit elements; how exact they have to be, the bound alone decides.
A program may use at most 64 MiB of HBM per device.

v0:
```python
import jax
import jax.numpy as jnp
from jax import lax
from jax.sharding import PartitionSpec as P

exact_mode = lax.Precision.HIGHEST


def shifted(value, axis, steps):
    count = lax.axis_size(axis)
    initial, last = (max(0, -steps), min(count, count - steps))
    return lax.ppermute(value, axis, [(source, source + steps) for source in range(initial, last)])


def build_model(block_mask, jump_logit, leave_rate, emit_logit, prior_logit):
    state_count = jump_logit.shape[0]
    block_width = state_count // block_mask.shape[0]
    block_grid = jnp.repeat(jnp.repeat(block_mask, block_width, axis=0), block_width, axis=1)
    block_ids = jnp.arange(state_count, dtype=jnp.int32) // block_width
    diagonal_blocks = (block_ids[:, None] == block_ids[None, :]).astype(jnp.int32)
    allowed = jnp.maximum(block_grid, diagonal_blocks)
    weights = jnp.where(allowed > 0, jnp.exp(jump_logit), 0.0)
    jump_matrix = weights / jnp.sum(weights, axis=1, keepdims=True)
    staying = jnp.eye(state_count, dtype=jump_logit.dtype) * (1.0 - leave_rate)[:, None]
    transition = staying + leave_rate[:, None] * jump_matrix
    emit_weight = jnp.exp(emit_logit)
    emission = emit_weight / jnp.sum(emit_weight, axis=0, keepdims=True)
    prior_weight = jnp.exp(prior_logit)
    initial_dist = prior_weight / jnp.sum(prior_weight)
    return (transition, emission, initial_dist)


def forward_backward(transition, likelihood, opening, closing):

    def forward_step(state_vec, emitted):
        advanced = jnp.dot(state_vec, transition, precision=exact_mode) * emitted
        advanced = advanced / jnp.sum(advanced)
        return (advanced, advanced)

    def backward_step(state_vec, emitted):
        previous = jnp.dot(transition, emitted * state_vec, precision=exact_mode)
        previous = previous / jnp.sum(previous)
        return (previous, state_vec)

    unused, alphas = lax.scan(forward_step, opening, likelihood)
    first_beta, later_betas = lax.scan(backward_step, closing, likelihood[1:], reverse=True)
    beta_rows = jnp.concatenate([first_beta[None, :], later_betas], axis=0)
    posterior = alphas * beta_rows
    return posterior * (transition.shape[0] / jnp.sum(posterior, axis=1, keepdims=True))


def whole_matrix(own_part, own_scale):
    pieces, scales = (
        lax.all_gather(own_part, "state", axis=0, tiled=True),
        lax.all_gather(own_scale[None], "state", axis=0, tiled=True),
    )
    piece_count = scales.shape[0]
    row_count = own_part.shape[0]
    largest = jnp.max(scales)
    factors = jnp.exp(scales - largest)
    stacked = pieces.reshape(piece_count, row_count, -1) * factors[:, None, None]
    return (stacked.reshape(piece_count * row_count, -1), largest)


def edge_vectors(own_vec, own_scale):
    pieces, scales = (
        lax.all_gather(own_vec[None, :], "state", axis=0, tiled=True),
        lax.all_gather(own_scale[None], "state", axis=0, tiled=True),
    )
    factors = jnp.exp(scales - jnp.max(scales))
    return pieces * factors[:, None]


def shards(observed, block_mask, jump_logit, leave_rate, emit_logit, prior_logit):
    transition, emission, initial_dist = build_model(
        block_mask, jump_logit, leave_rate, emit_logit, prior_logit
    )
    state_count = transition.shape[0]
    panel_count = lax.axis_size("state")
    row_count = state_count // panel_count
    panel_index = lax.axis_index("state")
    shard_count = lax.axis_size("tm")
    shard_id = lax.axis_index("tm")
    likelihood = jnp.take(emission, observed, axis=0)
    row_start = panel_index * row_count
    own_rows = lax.dynamic_slice_in_dim(transition, row_start, row_count, 0)
    opening_part = own_rows * likelihood[0][None, :]
    opening_max = jnp.max(opening_part)

    def advance(carried, emitted):
        product_part, log_scale = carried
        advanced = jnp.dot(product_part, transition, precision=exact_mode) * emitted[None, :]
        largest = jnp.max(advanced)
        return ((advanced / largest, log_scale + jnp.log(largest)), None)

    (own_part, own_scale), unused = lax.scan(
        advance, (opening_part / opening_max, jnp.log(opening_max)), likelihood[1:]
    )
    rounds = shard_count.bit_length() - 1
    identity_part = (
        jnp.arange(state_count)[None, :] == (row_start + jnp.arange(row_count))[:, None]
    ).astype(jnp.float32)
    arrived, arrived_scale = shifted((own_part, own_scale[None]), "tm", 1)
    at_first = shard_id == 0
    window = jnp.where(at_first, identity_part, arrived)
    window_scale = jnp.where(at_first, 0.0, arrived_scale[0])
    for round_index in range(rounds):
        distance = 1 << round_index
        earlier, earlier_scale = shifted((window, window_scale[None]), "tm", distance)
        whole, whole_scale = whole_matrix(window, window_scale)
        merged = jnp.dot(earlier, whole, precision=exact_mode)
        unchanged = shard_id < distance
        largest = jnp.where(unchanged, 1.0, jnp.max(merged))
        window = jnp.where(unchanged, window, merged / largest)
        window_scale = jnp.where(
            unchanged, window_scale, earlier_scale[0] + whole_scale + jnp.log(largest)
        )
    own_prior = lax.dynamic_slice_in_dim(initial_dist, row_start, row_count, 0)
    partial_vec = jnp.dot(own_prior, window, precision=exact_mode)
    incoming = jnp.sum(edge_vectors(partial_vec, window_scale), axis=0)
    incoming = incoming / jnp.sum(incoming)
    arrived, arrived_scale = shifted((own_part, own_scale[None]), "tm", -1)
    at_last = shard_id == shard_count - 1
    window = jnp.where(at_last, identity_part, arrived)
    window_scale = jnp.where(at_last, 0.0, arrived_scale[0])
    for round_index in range(rounds):
        distance = 1 << round_index
        later_part, later_scale = shifted((window, window_scale[None]), "tm", -distance)
        whole, whole_scale = whole_matrix(later_part, later_scale[0])
        merged = jnp.dot(window, whole, precision=exact_mode)
        unchanged = shard_id + distance >= shard_count
        largest = jnp.where(unchanged, 1.0, jnp.max(merged))
        window = jnp.where(unchanged, window, merged / largest)
        window_scale = jnp.where(
            unchanged, window_scale, window_scale + whole_scale + jnp.log(largest)
        )
    row_sums = jnp.sum(window, axis=1)
    outgoing = edge_vectors(row_sums, window_scale).reshape(-1)
    outgoing = outgoing / jnp.sum(outgoing)
    posterior = forward_backward(transition, likelihood, incoming, outgoing)
    column_count = state_count // panel_count
    return lax.dynamic_slice_in_dim(posterior, panel_index * column_count, column_count, 1)


def solution(mesh):
    return jax.shard_map(
        shards,
        mesh=mesh,
        in_specs=(P(("groups", "tm")), P(), P(), P(), P(), P()),
        out_specs=P(("groups", "tm"), "state"),
        check_vma=False,
    )
```

profile of v0, /device:TPU:0, one launch (start us, length us, event | category | flops | bytes accessed | tf_op | source)
XLA Modules:
  0.0 453.7 jit_solution(12747032921515535558)
XLA Ops:
  7.2 1.6 copy.20
  14.3 101.6 %while.40 = (s32[]{:T(128)}, f32[256,512]{1,0:T(8,128)S(1)}, f32[]{:T(128)}, f32[512,512]{1,0:T(8,128)S(1)}, f32[31,512]{1,0:T(8,128)S(1)}, /*index=5*/s32[]{:T(128)}) while((s32[]{:T(128)}, f32[256,512]{1,0:T(8,128)S(1)}, f32[]{:T(128)}, f32[512,512]{1,0:T(8,128)S(1)}, f32[31,512]{1,0:T(8,128)S(1)}, /*index=5*/s32[]{:T(128)}) %tuple.84), condition=%wide.region_6.7_spmd, body=%wide.region_4.6_spmd.sunk | while | flops 805699584 | bytes 3151973 | solution.py:96
  14.4 1.8 fusion.68
  17.6 1.8 fusion.68
  20.9 1.8 fusion.68
  24.2 1.8 fusion.68
  27.5 1.7 fusion.68
  30.7 1.8 fusion.68
  34.0 1.8 fusion.68
  37.3 1.8 fusion.68
  40.6 1.7 fusion.68
  43.9 1.8 fusion.68
  47.1 1.8 fusion.68
  50.4 1.8 fusion.68
  53.7 1.7 fusion.68
  57.0 1.8 fusion.68
  60.2 1.8 fusion.68
  63.5 1.8 fusion.68
  66.8 1.7 fusion.68
  70.1 1.8 fusion.68
  73.4 1.8 fusion.68
  76.6 1.8 fusion.68
  79.9 1.7 fusion.68
  83.2 1.8 fusion.68
  86.5 1.8 fusion.68
  89.8 1.8 fusion.68
  93.0 1.7 fusion.68
  96.3 1.8 fusion.68
  99.6 1.8 fusion.68
  102.9 1.8 fusion.68
  106.1 1.7 fusion.68
  109.4 1.8 fusion.68
  112.7 1.8 fusion.68
  115.9 4.9 %collective-permute-start = (f32[256,512]{1,0:T(8,128)S(1)}, f32[256,512]{1,0:T(8,128)S(1)}, u32[]{:S(2)}, u32[]{:S(2)}) collective-permute-start(f32[256,512]{1,0:T(8,128)S(1)} %get-tuple-element.164), channel_id=1, source_target_pairs={{0,2},{2,4},{4,6},{6,8},{8,10},{10,12},{12,14},{1,3},{3,5},{5,7},{... | collective-permute-start | bytes 1572872 | tf_op jit(solution)/shard_map/ppermute | solution.py:12
  122.2 21.0 %collective-permute-done = f32[256,512]{1,0:T(8,128)S(1)} collective-permute-done((f32[256,512]{1,0:T(8,128)S(1)}, f32[256,512]{1,0:T(8,128)S(1)}, u32[]{:S(2)}, u32[]{:S(2)}) %collective-permute-start) | collective-permute-done | bytes 524320 | tf_op jit(solution)/shard_map/ppermute | solution.py:12
  144.3 1.4 collective-permute-start.9
  147.0 15.6 %collective-permute-start.2 = (f32[1]{0:T(128)}, f32[1]{0:T(128)}, u32[]{:S(2)}, u32[]{:S(2)}) collective-permute-start(f32[1]{0:T(128)} %bitcast.13), channel_id=1, source_target_pairs={{0,2},{2,4},{4,6},{6,8},{8,10},{10,12},{12,14},{1,3},{3,5},{5,7},{... | collective-permute-start | bytes 20 | tf_op jit(solution)/shard_map/ppermute | solution.py:12
  167.2 4.2 collective-permute-done.11
  172.7 2.4 all-reduce.11
  176.5 4.8 %collective-permute-start.1 = (f32[256,512]{1,0:T(8,128)S(1)}, f32[256,512]{1,0:T(8,128)S(1)}, u32[]{:S(2)}, u32[]{:S(2)}) collective-permute-start(f32[256,512]{1,0:T(8,128)S(1)} %copy-done.1), channel_id=1, source_target_pairs={{0,2},{2,4},{4,6},{6,8},{8,10},{10,12},{12,14},{1,3},{3,5},{5,7},{... | collective-permute-start | bytes 1572872 | tf_op jit(solution)/shard_map/ppermute | solution.py:12
  183.8 9.0 %collective-permute-done.1 = f32[256,512]{1,0:T(8,128)S(1)} collective-permute-done((f32[256,512]{1,0:T(8,128)S(1)}, f32[256,512]{1,0:T(8,128)S(1)}, u32[]{:S(2)}, u32[]{:S(2)}) %collective-permute-start.1) | collective-permute-done | bytes 524320 | tf_op jit(solution)/shard_map/ppermute | solution.py:12
  193.6 3.2 fusion.35
  198.4 3.0 fusion.36
  202.2 1.4 collective-permute-start.12
  203.6 5.7 %collective-permute-start.4 = (f32[1]{0:T(128)}, f32[1]{0:T(128)}, u32[]{:S(2)}, u32[]{:S(2)}) collective-permute-start(f32[1]{0:T(128)} %bitcast.15), channel_id=1, source_target_pairs={{0,2},{2,4},{4,6},{6,8},{8,10},{10,12},{12,14},{1,3},{3,5},{5,7},{... | collective-permute-start | bytes 20 | tf_op jit(solution)/shard_map/ppermute | solution.py:12
  213.4 5.8 %collective-permute-done.13 = f32[1]{0:T(128)} collective-permute-done((f32[1]{0:T(128)}, f32[1]{0:T(128)}, u32[]{:S(2)}, u32[]{:S(2)}) %collective-permute-start.13) | collective-permute-done | bytes 36 | tf_op jit(solution)/shard_map/ppermute | solution.py:12
  220.6 3.9 collective-permute-start.3
  224.5 2.5 all-reduce.10
  230.7 2.8 collective-permute-done.3
  234.3 3.3 fusion.37
  239.2 3.0 fusion.38
  242.9 1.4 collective-permute-start.14
  245.8 5.7 %collective-permute-start.6 = (f32[1]{0:T(128)}, f32[1]{0:T(128)}, u32[]{:S(2)}, u32[]{:S(2)}) collective-permute-start(f32[1]{0:T(128)} %bitcast.18), channel_id=1, source_target_pairs={{0,4},{2,6},{4,8},{6,10},{8,12},{10,14},{1,5},{3,7},{5,9},{7,11},{... | collective-permute-start | bytes 20 | tf_op jit(solution)/shard_map/ppermute | solution.py:12
  253.6 6.8 %collective-permute-start.7 = (f32[1]{0:T(128)}, f32[1]{0:T(128)}, u32[]{:S(2)}, u32[]{:S(2)}) collective-permute-start(f32[1]{0:T(128)} %bitcast.20), channel_id=1, source_target_pairs={{0,8},{2,10},{4,12},{6,14},{1,9},{3,11},{5,13},{7,15},{16,24},{18,... | collective-permute-start | bytes 20 | tf_op jit(solution)/shard_map/ppermute | solution.py:12
  262.4 6.8 %collective-permute-done.15 = f32[1]{0:T(128)} collective-permute-done((f32[1]{0:T(128)}, f32[1]{0:T(128)}, u32[]{:S(2)}, u32[]{:S(2)}) %collective-permute-start.15) | collective-permute-done | bytes 36 | tf_op jit(solution)/shard_map/ppermute | solution.py:12
  271.9 2.7 all-reduce.9
  279.8 2.1 collective-permute-done.5
  281.9 3.1 fusion.39
  286.7 3.1 fusion.40
  291.2 1.8 all-gather.2
  293.0 2.5 all-reduce.8
  297.0 1.8 all-gather.3
  300.3 75.8 %while.42 = (s32[]{:T(128)}, f32[512]{0:T(512)S(1)}, f32[31,512]{1,0:T(8,128)S(1)}, f32[31,512]{1,0:T(8,128)S(1)}, f32[512,512]{1,0:T(8,128)S(1)}, /*index=5*/s32[]{:T(128)}, s32[]{:T(128)}, f32[]{:T(128)}, s32[]{:T(128)}) while((s32[]{:T(128)}, f32[512]{0:T(512)S(1)}, f32[31,512]{1,0:T(8,128)S(1)}, f32[31,512]{1,0:T(8,128)S(1)}, ...), condition=%wide.region_30.31_spmd, body=%wide.region_28.30_spmd.sunk | while | flops 3147266 | bytes 1073277 | solution.py:46
  378.9 67.1 %while.41 = (s32[]{:T(128)}, f32[512]{0:T(512)S(1)}, f32[32,512]{1,0:T(8,128)S(1)}, f32[512,512]{1,0:T(8,128)S(1)}, f32[32,512]{1,0:T(8,128)S(1)}, /*index=5*/s32[]{:T(128)}, s32[]{:T(128)}) while((s32[]{:T(128)}, f32[512]{0:T(512)S(1)}, f32[32,512]{1,0:T(8,128)S(1)}, f32[512,512]{1,0:T(8,128)S(1)}, f32[32,512]{1,0:T(8,128)S(1)}, ...), condition=%wide.region_18.19_spmd, body=%wide.region_16.18_spmd.sunk | while | flops 3147265 | bytes 1071197 | solution.py:45
  (554 shorter events, 209.5 us)
Async XLA Ops:
  6.5 2.3 copy-start
  6.5 186.3 %all-gather.11.cloned.1.call-start = ((), (), s32[]{:S(2)}) async-start(), calls=%async_computation | async-start | bytes 1572864 | tf_op jit(solution)/shard_map/all_gather | solution.py:54
  6.5 0.7 copy-start.12
  8.8 1.1 copy-start.3
  8.8 0.7 copy-start.10
  115.9 27.3 %collective-permute-start = (f32[256,512]{1,0:T(8,128)S(1)}, f32[256,512]{1,0:T(8,128)S(1)}, u32[]{:S(2)}, u32[]{:S(2)}) collective-permute-start(f32[256,512]{1,0:T(8,128)S(1)} %get-tuple-element.164), channel_id=1, source_target_pairs={{0,2},{2,4},{4,6},{6,8},{8,10},{10,12},{12,14},{1,3},{3,5},{5,7},{... | collective-permute-start | bytes 1572872 | tf_op jit(solution)/shard_map/ppermute | solution.py:12
  120.9 22.4 %collective-permute-start.8 = (f32[256,512]{1,0:T(8,128)S(1)}, f32[256,512]{1,0:T(8,128)S(1)}, u32[]{:S(2)}, u32[]{:S(2)}) collective-permute-start(f32[256,512]{1,0:T(8,128)S(1)} %get-tuple-element.164), channel_id=1, source_target_pairs={{2,0},{4,2},{6,4},{8,6},{10,8},{12,10},{14,12},{3,1},{5,3},{7,5},{... | collective-permute-start | bytes 1572872 | tf_op jit(solution)/shard_map/ppermute | solution.py:12
  144.2 32.3 %copy-start.1 = (f32[256,512]{1,0:T(8,128)S(1)}, f32[256,512]{1,0:T(8,128)}, u32[]{:S(2)}) copy-start(f32[256,512]{1,0:T(8,128)} %get-tuple-element.261) | copy-start | bytes 1572868
  144.2 54.2 %all-gather.17.cloned.1.call-start = ((), (), s32[]{:S(2)}) async-start(), calls=%async_computation.3 | async-start | bytes 1572864 | tf_op jit(solution)/shard_map/all_gather | solution.py:54
  144.3 37.1 %collective-permute-start.9 = (f32[256,512]{1,0:T(8,128)S(1)}, f32[256,512]{1,0:T(8,128)S(1)}, u32[]{:S(2)}, u32[]{:S(2)}) collective-permute-start(f32[256,512]{1,0:T(8,128)S(1)} %get-tuple-element.260), channel_id=1, source_target_pairs={{2,0},{4,2},{6,4},{8,6},{10,8},{12,10},{14,12},{3,1},{5,3},{7,5},{... | collective-permute-start | bytes 1572872 | tf_op jit(solution)/shard_map/ppermute | solution.py:12
  145.7 18.1 %collective-permute-start.10 = (f32[1]{0:T(128)}, f32[1]{0:T(128)}, u32[]{:S(2)}, u32[]{:S(2)}) collective-permute-start(f32[1]{0:T(128)} %bitcast.13), channel_id=1, source_target_pairs={{2,0},{4,2},{6,4},{8,6},{10,8},{12,10},{14,12},{3,1},{5,3},{7,5},{... | collective-permute-start | bytes 20 | tf_op jit(solution)/shard_map/ppermute | solution.py:12
  147.0 18.8 %collective-permute-start.2 = (f32[1]{0:T(128)}, f32[1]{0:T(128)}, u32[]{:S(2)}, u32[]{:S(2)}) collective-permute-start(f32[1]{0:T(128)} %bitcast.13), channel_id=1, source_target_pairs={{0,2},{2,4},{4,6},{6,8},{8,10},{10,12},{12,14},{1,3},{3,5},{5,7},{... | collective-permute-start | bytes 20 | tf_op jit(solution)/shard_map/ppermute | solution.py:12
  162.6 0.7 copy-start.13
  164.5 6.8 %collective-permute-start.11 = (f32[1]{0:T(128)}, f32[1]{0:T(128)}, u32[]{:S(2)}, u32[]{:S(2)}) collective-permute-start(f32[1]{0:T(128)} %bitcast.26), channel_id=1, source_target_pairs={{2,0},{4,2},{6,4},{8,6},{10,8},{12,10},{14,12},{3,1},{5,3},{7,5},{... | collective-permute-start | bytes 20 | tf_op jit(solution)/shard_map/ppermute | solution.py:12
  176.5 16.3 %collective-permute-start.1 = (f32[256,512]{1,0:T(8,128)S(1)}, f32[256,512]{1,0:T(8,128)S(1)}, u32[]{:S(2)}, u32[]{:S(2)}) collective-permute-start(f32[256,512]{1,0:T(8,128)S(1)} %copy-done.1), channel_id=1, source_target_pairs={{0,2},{2,4},{4,6},{6,8},{8,10},{10,12},{12,14},{1,3},{3,5},{5,7},{... | collective-permute-start | bytes 1572872 | tf_op jit(solution)/shard_map/ppermute | solution.py:12
  181.3 0.8 copy-start.7
  182.2 51.3 %all-gather.13.cloned.1.call-start = ((), (), s32[]{:S(2)}) async-start(), calls=%async_computation.1 | async-start | bytes 1572864 | tf_op jit(solution)/shard_map/all_gather | solution.py:54
  192.8 0.8 copy-start.9
  198.3 40.8 %all-gather.19.cloned.1.call-start = ((), (), s32[]{:S(2)}) async-start(), calls=%async_computation.4 | async-start | bytes 1572864 | tf_op jit(solution)/shard_map/all_gather | solution.py:54
  202.1 18.5 %copy-start.2 = (f32[256,512]{1,0:T(8,128)S(1)}, f32[256,512]{1,0:T(8,128)}, u32[]{:S(2)}) copy-start(f32[256,512]{1,0:T(8,128)} %divide_select_fusion.3) | copy-start | bytes 1572868
  202.2 26.1 %collective-permute-start.12 = (f32[256,512]{1,0:T(8,128)S(1)}, f32[256,512]{1,0:T(8,128)S(1)}, u32[]{:S(2)}, u32[]{:S(2)}) collective-permute-start(f32[256,512]{1,0:T(8,128)S(1)} %divide_select_fusion.1), channel_id=1, source_target_pairs={{4,0},{6,2},{8,4},{10,6},{12,8},{14,10},{5,1},{7,3},{9,5},{11,7},{... | collective-permute-start | bytes 1572872 | tf_op jit(solution)/shard_map/ppermute | solution.py:12
  203.6 6.3 %collective-permute-start.4 = (f32[1]{0:T(128)}, f32[1]{0:T(128)}, u32[]{:S(2)}, u32[]{:S(2)}) collective-permute-start(f32[1]{0:T(128)} %bitcast.15), channel_id=1, source_target_pairs={{0,2},{2,4},{4,6},{6,8},{8,10},{10,12},{12,14},{1,3},{3,5},{5,7},{... | collective-permute-start | bytes 20 | tf_op jit(solution)/shard_map/ppermute | solution.py:12
  212.1 7.1 %collective-permute-start.13 = (f32[1]{0:T(128)}, f32[1]{0:T(128)}, u32[]{:S(2)}, u32[]{:S(2)}) collective-permute-start(f32[1]{0:T(128)} %bitcast.27), channel_id=1, source_target_pairs={{4,0},{6,2},{8,4},{10,6},{12,8},{14,10},{5,1},{7,3},{9,5},{11,7},{... | collective-permute-start | bytes 20 | tf_op jit(solution)/shard_map/ppermute | solution.py:12
  220.6 12.9 %collective-permute-start.3 = (f32[256,512]{1,0:T(8,128)S(1)}, f32[256,512]{1,0:T(8,128)S(1)}, u32[]{:S(2)}, u32[]{:S(2)}) collective-permute-start(f32[256,512]{1,0:T(8,128)S(1)} %copy-done.2), channel_id=1, source_target_pairs={{0,4},{2,6},{4,8},{6,10},{8,12},{10,14},{1,5},{3,7},{5,9},{7,11},{... | collective-permute-start | bytes 1572872 | tf_op jit(solution)/shard_map/ppermute | solution.py:12
  228.3 0.8 copy-start.6
  229.1 52.8 %all-gather.15.cloned.1.call-start = ((), (), s32[]{:S(2)}) async-start(), calls=%async_computation.2 | async-start | bytes 1572864 | tf_op jit(solution)/shard_map/all_gather | solution.py:54
  233.5 0.8 copy-start.8
  239.1 47.6 %all-gather.21.cloned.1.call-start = ((), (), s32[]{:S(2)}) async-start(), calls=%async_computation.5 | async-start | bytes 1572864 | tf_op jit(solution)/shard_map/all_gather | solution.py:54
  242.8 1.6 copy-start.11
  242.8 27.7 %copy-start.4 = (f32[256,512]{1,0:T(8,128)S(1)}, f32[256,512]{1,0:T(8,128)}, u32[]{:S(2)}) copy-start(f32[256,512]{1,0:T(8,128)} %divide_select_fusion.2) | copy-start | bytes 1572868
  242.9 32.8 %collective-permute-start.14 = (f32[256,512]{1,0:T(8,128)S(1)}, f32[256,512]{1,0:T(8,128)S(1)}, u32[]{:S(2)}, u32[]{:S(2)}) collective-permute-start(f32[256,512]{1,0:T(8,128)S(1)} %divide_select_fusion), channel_id=1, source_target_pairs={{8,0},{10,2},{12,4},{14,6},{9,1},{11,3},{13,5},{15,7},{24,16},{26,... | collective-permute-start | bytes 1572872 | tf_op jit(solution)/shard_map/ppermute | solution.py:12
  245.8 6.4 %collective-permute-start.6 = (f32[1]{0:T(128)}, f32[1]{0:T(128)}, u32[]{:S(2)}, u32[]{:S(2)}) collective-permute-start(f32[1]{0:T(128)} %bitcast.18), channel_id=1, source_target_pairs={{0,4},{2,6},{4,8},{6,10},{8,12},{10,14},{1,5},{3,7},{5,9},{7,11},{... | collective-permute-start | bytes 20 | tf_op jit(solution)/shard_map/ppermute | solution.py:12
  253.6 24.3 %collective-permute-start.7 = (f32[1]{0:T(128)}, f32[1]{0:T(128)}, u32[]{:S(2)}, u32[]{:S(2)}) collective-permute-start(f32[1]{0:T(128)} %bitcast.20), channel_id=1, source_target_pairs={{0,8},{2,10},{4,12},{6,14},{1,9},{3,11},{5,13},{7,15},{16,24},{18,... | collective-permute-start | bytes 20 | tf_op jit(solution)/shard_map/ppermute | solution.py:12
  261.1 8.1 %collective-permute-start.15 = (f32[1]{0:T(128)}, f32[1]{0:T(128)}, u32[]{:S(2)}, u32[]{:S(2)}) collective-permute-start(f32[1]{0:T(128)} %bitcast.28), channel_id=1, source_target_pairs={{8,0},{10,2},{12,4},{14,6},{9,1},{11,3},{13,5},{15,7},{24,16},{26,... | collective-permute-start | bytes 20 | tf_op jit(solution)/shard_map/ppermute | solution.py:12
  270.5 11.4 %collective-permute-start.5 = (f32[256,512]{1,0:T(8,128)S(1)}, f32[256,512]{1,0:T(8,128)S(1)}, u32[]{:S(2)}, u32[]{:S(2)}) collective-permute-start(f32[256,512]{1,0:T(8,128)S(1)} %copy-done.4), channel_id=1, source_target_pairs={{0,8},{2,10},{4,12},{6,14},{1,9},{3,11},{5,13},{7,15},{16,24},{18,... | collective-permute-start | bytes 1572872 | tf_op jit(solution)/shard_map/ppermute | solution.py:12
  275.8 0.8 copy-start.5
Sparse Core Ops, SparseCore 0:
  144.3 11.1 all-gather.10
  182.3 8.9 all-gather.16
  198.4 10.8 all-gather.12
  229.3 7.7 all-gather.18
  239.2 9.5 all-gather.14
  276.7 7.4 all-gather.20
where the time goes:
time: 462 us; the launch traced here: 454 us
  other arithmetic  132 us (29%)
  matrix products  122 us (26%)
  starting transfers between devices  59.8 us (13%)
  waiting for transfers between devices  51.9 us (11%)
  loops' own time  26.7 us (6%)
  between operations  26.1 us (6%)
  local copies, waits for them, and re-layouts  21.5 us (5%)
  blocking collectives  13.6 us (3%)
    ppermute x16, starting transfers between devices, shifted(): lax.ppermute(value, axis, [(source, source + steps) for source in range(i...  59.6 us
    dot_general x31, matrix products, advance(): jnp.dot(product_part, transition, precision=exact_mode) * emitted[None, :]  54.3 us
    ppermute x16, waiting for transfers between devices, shifted(): lax.ppermute(value, axis, [(source, source + steps) for source in range(i...  51.7 us
    dot_general x31, matrix products, backward_step(): previous = jnp.dot(transition, emitted * state_vec, precision=exact_mode)  29.7 us
    another operation x1, loops' own time, shards(): lax.scan(advance, (opening_part / opening_max, jnp.log(opening_max)), lik...  24 us
    div x31, other arithmetic, advance(): return ((advanced / largest, log_scale + jnp.log(largest)), None)  23 us
    reduce_sum x32, other arithmetic, forward_step(): advanced = advanced / jnp.sum(advanced)  22.1 us
    div x32, other arithmetic, forward_step(): advanced = advanced / jnp.sum(advanced)  22.1 us
  transfers between devices with their start and end apart: 22, of which 7 were waited for; matrix products, arithmetic and copies ran while one was open for 8% of the time, Pallas kernels for 0%

commit v1 on v0

v1 whole, which is shorter than its diff:
```python
import functools

import jax
import jax.numpy as jnp
from jax import lax
from jax.experimental import pallas as pl
from jax.experimental.pallas import tpu as pltpu
from jax.sharding import PartitionSpec as P

MESH = pl.DeviceIdType.MESH
F32 = jnp.float32
BF16 = jnp.bfloat16
CHUNKS = 2


def split(x):
    high = x.astype(BF16).astype(F32)
    return high, x - high


def pair(x):
    high, low = split(x)
    row = lax.broadcasted_iota(jnp.int32, (16, x.shape[1]), 0)
    return jnp.where(row == 0, high, jnp.where(row == 1, low, 0.0)).astype(BF16)


def times(x, weights):
    out = jnp.dot(pair(x), weights, preferred_element_type=F32)
    n = out.shape[1] // 2
    return (out[0:1, :n] + out[1:2, :n]) + (out[0:1, n:] + out[1:2, n:])


def put_pieces(ref, x):
    high, low = split(x)
    n = x.shape[1]
    ref[:, :n] = high.astype(BF16)
    ref[:, n:] = low.astype(BF16)


def kernel(
    shard_count,
    observed_ref, mask_ref, jump_ref, leave_ref, emit_ref, prior_ref,
    out_ref,
    moves, fwd_w, bwd_w, symbols, lik, part, logs, chain_f, chain_b,
    peak_out, peak_in, fwd_out, fwd_in, bwd_out, bwd_in, alphas, betas,
    peak_sems, fwd_send, fwd_recv, bwd_send, bwd_recv,
):
    shard = lax.axis_index("tm")
    core = lax.axis_index("state")
    states = jump_ref.shape[0]
    half = states // 2
    steps = lik.shape[0]
    first, last = shard == 0, shard == shard_count - 1

    barrier = pltpu.get_barrier_semaphore()
    pl.semaphore_signal(barrier, inc=1, device_id={"state": 1 - core}, device_id_type=MESH)

    @pl.when(jnp.logical_not(first))
    def _():
        for c in range(2):
            pl.semaphore_signal(
                barrier, inc=1, device_id={"tm": shard - 1, "state": c}, device_id_type=MESH
            )

    @pl.when(jnp.logical_not(last))
    def _():
        for c in range(2):
            pl.semaphore_signal(
                barrier, inc=1, device_id={"tm": shard + 1, "state": c}, device_id_type=MESH
            )

    width = states // mask_ref.shape[0]
    blocks = mask_ref.shape[0]
    spread = (
        lax.broadcasted_iota(jnp.int32, (states, blocks), 0) // width
        == lax.broadcasted_iota(jnp.int32, (states, blocks), 1)
    ).astype(F32).astype(BF16)
    spread_t = (
        lax.broadcasted_iota(jnp.int32, (blocks, states), 1) // width
        == lax.broadcasted_iota(jnp.int32, (blocks, states), 0)
    ).astype(F32).astype(BF16)
    eye = lax.broadcasted_iota(jnp.int32, (blocks, blocks), 0) == lax.broadcasted_iota(
        jnp.int32, (blocks, blocks), 1
    )
    grid = jnp.where(eye, 1.0, mask_ref[...].astype(F32)).astype(BF16)
    tall = jnp.dot(spread, grid, preferred_element_type=F32).astype(BF16)
    allowed = jnp.dot(tall, spread_t, preferred_element_type=F32)
    weights = jnp.where(allowed > 0.5, jnp.exp(jump_ref[...]), 0.0)
    leave = leave_ref[...]
    stay = 1.0 - leave
    leave_col = jnp.transpose(jnp.broadcast_to(leave, (128, states)))[:, 0:1]
    off = weights * (leave_col / jnp.sum(weights, axis=1, keepdims=True))
    moves[...] = off
    put_pieces(fwd_w, off)
    put_pieces(bwd_w, jnp.transpose(off))

    emit = jnp.exp(emit_ref[...])
    symbols[...] = emit
    share = 1.0 / jnp.sum(emit, axis=0, keepdims=True)
    for t in range(steps):
        lik[t:t + 1, :] = symbols[pl.ds(observed_ref[t], 1), :]
    rows = lik[...] * share
    lik[...] = rows / jnp.max(rows, axis=1, keepdims=True)

    own = lax.broadcasted_iota(jnp.int32, (half, states), 0) + core * half
    diagonal = own == lax.broadcasted_iota(jnp.int32, (half, states), 1)
    start = pl.multiple_of(core * half, half)
    part[...] = (moves[pl.ds(start, half), :] + jnp.where(diagonal, stay, 0.0)) * lik[0:1, :]
    logs[...] = jnp.zeros_like(logs)
    size = half // CHUNKS

    def advance(t, rescale):
        emitted = lik[pl.ds(t, 1), :]
        for h in range(CHUNKS):
            at = slice(h * size, (h + 1) * size)
            a = part[at, :]
            high, low = split(a)
            high, low = high.astype(BF16), low.astype(BF16)
            both = jnp.dot(
                jnp.concatenate([high, low], axis=0), fwd_w[:, :states],
                preferred_element_type=F32,
            )
            rest = jnp.dot(high, fwd_w[:, states:], preferred_element_type=F32)
            new = (a * stay + (both[:size] + (both[size:] + rest))) * emitted
            if rescale:
                peak = jnp.max(a, axis=1, keepdims=True)
                new = new * (1.0 / peak)
                logs[at, :] = logs[at, :] + jnp.log(peak)
            part[at, :] = new

    def two(i, carry):
        advance(1 + 2 * i, True)
        advance(2 + 2 * i, False)
        return carry

    lax.fori_loop(0, (steps - 1) // 2, two, 0)
    if (steps - 1) % 2:
        advance(steps - 1, True)

    final_log = logs[...]
    own_peak = jnp.max(final_log + jnp.log(jnp.max(part[...], axis=1, keepdims=True)))
    peak_out[...] = jnp.full(peak_out.shape, own_peak, F32)
    neighbours = 1 + 2 * (
        jnp.where(first, 0, 1).astype(jnp.int32) + jnp.where(last, 0, 1).astype(jnp.int32)
    )
    pl.semaphore_wait(barrier, neighbours)
    peak_copy = pltpu.make_async_remote_copy(
        src_ref=peak_out, dst_ref=peak_in, send_sem=peak_sems.at[0], recv_sem=peak_sems.at[1],
        device_id={"state": 1 - core}, device_id_type=MESH,
    )
    peak_copy.start()
    peak_copy.wait()
    top = jnp.maximum(peak_out[0:1, 0:1], peak_in[0:1, 0:1])
    whole = part[...] * jnp.exp(final_log - top)
    put_pieces(chain_f, whole)
    put_pieces(chain_b, jnp.transpose(whole))

    def fwd_copy(c):
        return pltpu.make_async_remote_copy(
            src_ref=fwd_out, dst_ref=fwd_in.at[core],
            send_sem=fwd_send.at[c], recv_sem=fwd_recv.at[core],
            device_id={"tm": shard + 1, "state": c}, device_id_type=MESH,
        )

    def bwd_copy(c):
        return pltpu.make_async_remote_copy(
            src_ref=bwd_out, dst_ref=bwd_in.at[core],
            send_sem=bwd_send.at[c], recv_sem=bwd_recv.at[core],
            device_id={"tm": shard - 1, "state": c}, device_id_type=MESH,
        )

    def fwd_arrival(c):
        return pltpu.make_async_remote_copy(
            src_ref=fwd_out, dst_ref=fwd_in.at[c],
            send_sem=fwd_send.at[c], recv_sem=fwd_recv.at[c],
            device_id={"state": 1 - core}, device_id_type=MESH,
        )

    def bwd_arrival(c):
        return pltpu.make_async_remote_copy(
            src_ref=bwd_out, dst_ref=bwd_in.at[c],
            send_sem=bwd_send.at[c], recv_sem=bwd_recv.at[c],
            device_id={"state": 1 - core}, device_id_type=MESH,
        )

    @pl.when(first)
    def _():
        fwd_in[0] = jnp.exp(prior_ref[...])
        fwd_in[1] = jnp.zeros((1, states), F32)

    @pl.when(last)
    def _():
        bwd_in[0] = jnp.ones((1, half), F32)
        bwd_in[1] = jnp.ones((1, half), F32)

    def forward():
        @pl.when(jnp.logical_not(first))
        def _():
            for c in range(2):
                fwd_arrival(c).wait_recv()

        @pl.when(jnp.logical_not(last))
        def _():
            v = fwd_in[0] + fwd_in[1]
            scale = 1.0 / jnp.max(v, axis=1, keepdims=True)
            mine = jnp.where(core == 0, v[:, :half], v[:, half:])
            fwd_out[...] = times(mine, chain_f[...]) * scale
            for c in range(2):
                fwd_copy(c).start()

    def backward():
        @pl.when(jnp.logical_not(last))
        def _():
            for c in range(2):
                bwd_arrival(c).wait_recv()

        @pl.when(jnp.logical_not(first))
        def _():
            w = jnp.concatenate([bwd_in[0], bwd_in[1]], axis=1)
            scale = 1.0 / jnp.max(w, axis=1, keepdims=True)
            bwd_out[...] = times(w, chain_b[...]) * scale
            for c in range(2):
                bwd_copy(c).start()

    early = shard < shard_count // 2

    @pl.when(early)
    def _():
        forward()
        backward()

    @pl.when(jnp.logical_not(early))
    def _():
        backward()
        forward()

    a = fwd_in[0] + fwd_in[1]
    a = a / jnp.max(a, axis=1, keepdims=True)
    b = jnp.concatenate([bwd_in[0], bwd_in[1]], axis=1)
    b = b / jnp.max(b, axis=1, keepdims=True)

    def walk(i, carry):
        a, b = carry
        emitted = lik[pl.ds(i, 1), :]
        scale = 1.0 / jnp.max(a, axis=1, keepdims=True)
        a_new = (a * stay + times(a, fwd_w[...])) * (emitted * scale)
        alphas[pl.ds(i, 1), :] = a_new
        t = steps - 1 - i
        betas[pl.ds(t, 1), :] = b
        x = b * lik[pl.ds(t, 1), :]
        scale = 1.0 / jnp.max(x, axis=1, keepdims=True)
        b_new = (x * stay + times(x, bwd_w[...])) * scale
        return a_new, b_new

    lax.fori_loop(0, steps, walk, (a, b))
    joint = alphas[...] * betas[...]
    factor = states / jnp.sum(joint, axis=1, keepdims=True)
    out_ref[...] = jnp.where(core == 0, joint[:, :half], joint[:, half:]) * factor

    @pl.when(jnp.logical_not(last))
    def _():
        for c in range(2):
            fwd_copy(c).wait_send()

    @pl.when(jnp.logical_not(first))
    def _():
        for c in range(2):
            bwd_copy(c).wait_send()


def shards(shard_count, observed, block_mask, jump_logit, leave_rate, emit_logit, prior_logit):
    states = jump_logit.shape[0]
    half = states // 2
    symbols = emit_logit.shape[0]
    steps = observed.shape[0]
    vmem = pl.BlockSpec(memory_space=pltpu.VMEM)
    return pl.pallas_call(
        functools.partial(kernel, shard_count),
        out_shape=jax.ShapeDtypeStruct((steps, half), F32),
        in_specs=[pl.BlockSpec(memory_space=pltpu.SMEM)] + [vmem] * 5,
        out_specs=vmem,
        scratch_shapes=[
            pltpu.VMEM((states, states), F32),
            pltpu.VMEM((states, 2 * states), BF16),
            pltpu.VMEM((states, 2 * states), BF16),
            pltpu.VMEM((symbols, states), F32),
            pltpu.VMEM((steps, states), F32),
            pltpu.VMEM((half, states), F32),
            pltpu.VMEM((half, 1), F32),
            pltpu.VMEM((half, 2 * states), BF16),
            pltpu.VMEM((states, 2 * half), BF16),
            pltpu.VMEM((1, 128), F32),
            pltpu.VMEM((1, 128), F32),
            pltpu.VMEM((1, states), F32),
            pltpu.VMEM((2, 1, states), F32),
            pltpu.VMEM((1, half), F32),
            pltpu.VMEM((2, 1, half), F32),
            pltpu.VMEM((steps, states), F32),
            pltpu.VMEM((steps, states), F32),
            pltpu.SemaphoreType.DMA((2,)),
            pltpu.SemaphoreType.DMA((2,)),
            pltpu.SemaphoreType.DMA((2,)),
            pltpu.SemaphoreType.DMA((2,)),
            pltpu.SemaphoreType.DMA((2,)),
        ],
        compiler_params=pltpu.CompilerParams(
            collective_id=0, has_side_effects=True, vmem_limit_bytes=40 * 1024 * 1024
        ),
    )(observed, block_mask, jump_logit, leave_rate[None, :], emit_logit, prior_logit[None, :])


def solution(mesh):
    return jax.shard_map(
        functools.partial(shards, mesh.shape["tm"]),
        mesh=mesh,
        in_specs=(P(("groups", "tm")), P(), P(), P(), P(), P()),
        out_specs=P(("groups", "tm"), "state"),
        check_vma=False,
    )
```

time: 462 us -> 61.1 us (0.13); the launches traced: 454 us -> 60.8 us
  other arithmetic: 132 us -> 0 us
  matrix products: 122 us -> 0 us
  starting transfers between devices: 59.8 us -> 0 us
  Pallas kernels: 0 us -> 55.8 us
  waiting for transfers between devices: 51.9 us -> 0 us
  loops' own time: 26.7 us -> 0 us
  between operations: 26.1 us -> 0.02 us
  local copies, waits for them, and re-layouts: 21.5 us -> 5 us
  blocking collectives: 13.6 us -> 0 us
    dot_general x101 -> x0, matrix products: 122 us -> none  [the longest x31 54.3 us: advance(): jnp.dot(product_part, transition, precision=exact_mode) * emitted[None, :]]
    div x99 -> x0, other arithmetic: 68.9 us -> none  [the longest x31 23 us: advance(): return ((advanced / largest, log_scale + jnp.log(largest)), None)]
    ppermute x16 -> x0, starting transfers between devices: 59.6 us -> none  [shifted(): lax.ppermute(value, axis, [(source, source + steps) for source in range(i...]
    pallas_call x0 -> x1, Pallas kernels: none -> 55.8 us  [shards(): pl.pallas_call(functools.partial(kernel, shard_count), out_shape=jax.Shap...]
    ppermute x16 -> x0, waiting for transfers between devices: 51.7 us -> none  [shifted(): lax.ppermute(value, axis, [(source, source + steps) for source in range(i...]
    reduce_sum x70 -> x0, other arithmetic: 46.8 us -> none  [the longest x32 22.1 us: forward_step(): advanced = advanced / jnp.sum(advanced)]
    another operation x3 -> x0, loops' own time: 26.7 us -> none  [the longest x1 24 us: shards(): lax.scan(advance, (opening_part / opening_max, jnp.log(opening_max)), lik...]
    unnamed x59 -> x13, local copies, waits for them, and re-layouts: 16.2 us -> 5 us
  transfers between devices with their start and end apart: 22 -> 0, of which waited for: 7 -> 0; matrix products, arithmetic and copies ran while one was open for 8% -> 0% of each run, Pallas kernels for 0% -> 0%
where the time goes in v1:
time: 61.1 us; the launch traced here: 60.8 us
  Pallas kernels  55.8 us (91%)
  local copies, waits for them, and re-layouts  5 us (8%)
    pallas_call x1, Pallas kernels, shards(): pl.pallas_call(functools.partial(kernel, shard_count), out_shape=jax.Shap...  55.8 us
    unnamed x13, local copies, waits for them, and re-layouts  5 us

profile of v1, /device:TPU:0, one launch (start us, length us, event | category | flops | bytes accessed | tf_op | source)
XLA Modules:
  0.0 60.8 jit_solution(7850913610602254388)
XLA Ops:
  0.0 0.0 copy-start.3
  0.0 0.0 copy-start.5
  0.0 0.7 %copy-done.3 = f32[512]{0:T(512)S(1)} copy-done((f32[512]{0:T(512)S(1)}, f32[512]{0:T(512)}, u32[]{:S(2)}) %copy-start.3) | copy-done | bytes 2072
  0.7 0.0 copy-done.5
  0.7 0.0 copy-start
  0.7 1.2 %copy-done = f32[512,512]{1,0:T(8,128)S(1)} copy-done((f32[512,512]{1,0:T(8,128)S(1)}, f32[512,512]{1,0:T(8,128)}, u32[]{:S(2)}) %copy-start) | copy-done | bytes 1048600
  1.9 0.0 copy-start.1
  1.9 1.0 %copy-done.1 = f32[256,512]{1,0:T(8,128)S(1)} copy-done((f32[256,512]{1,0:T(8,128)S(1)}, f32[256,512]{1,0:T(8,128)}, u32[]{:S(2)}) %copy-start.1) | copy-done | bytes 524312
  3.0 0.0 copy-start.2
  3.0 0.8 %copy-done.2 = s32[64,64]{1,0:T(8,128)S(1)} copy-done((s32[64,64]{1,0:T(8,128)S(1)}, s32[64,64]{1,0:T(8,128)}, u32[]{:S(2)}) %copy-start.2) | copy-done | bytes 16408
  3.7 0.0 copy-start.4
  3.7 0.7 %copy-done.4 = f32[512]{0:T(512)S(1)} copy-done((f32[512]{0:T(512)S(1)}, f32[512]{0:T(512)}, u32[]{:S(2)}) %copy-start.4) | copy-done | bytes 2072
  4.4 55.8 %shard_map.64 = f32[32,256]{1,0:T(8,128)S(1)} custom-call(s32[32]{0:T(128)S(1)} %copy-done.5, s32[64,64]{1,0:T(8,128)S(1)} %copy-done.2, f32[512,512]{1,0:T(8,128)S(1)} %copy-done, f32[1,512]{1,0:T(1,128)S(1)} %bitcast.2, f32[256,512]{1,0:T(8,128)S(1)} %copy-done.1, f32[1,512]{1,0:T(1,128)S(1)} %bitcast.3), custom_call_target="tpu_custom_call" | custom-call | tf_op jit(solution)/shard_map/pallas_call | solution.py:277
  60.2 0.6 %copy.8 = f32[32,256]{1,0:T(8,128)} copy(f32[32,256]{1,0:T(8,128)S(1)} %shard_map.64) | data formatting | bytes 65536
Async XLA Ops:
  0.0 0.7 %copy-start.3 = (f32[512]{0:T(512)S(1)}, f32[512]{0:T(512)}, u32[]{:S(2)}) copy-start(f32[512]{0:T(512)} %param.9) | copy-start | bytes 6148
  0.0 0.7 %copy-start.5 = (s32[32]{0:T(128)S(1)}, s32[32]{0:T(128)}, u32[]{:S(2)}) copy-start(s32[32]{0:T(128)} %observed_ref.1) | copy-start | bytes 388
  0.7 1.2 %copy-start = (f32[512,512]{1,0:T(8,128)S(1)}, f32[512,512]{1,0:T(8,128)}, u32[]{:S(2)}) copy-start(f32[512,512]{1,0:T(8,128)} %jump_ref.1) | copy-start | bytes 3145732
  1.9 1.0 %copy-start.1 = (f32[256,512]{1,0:T(8,128)S(1)}, f32[256,512]{1,0:T(8,128)}, u32[]{:S(2)}) copy-start(f32[256,512]{1,0:T(8,128)} %emit_ref.1) | copy-start | bytes 1572868
  3.0 0.8 %copy-start.2 = (s32[64,64]{1,0:T(8,128)S(1)}, s32[64,64]{1,0:T(8,128)}, u32[]{:S(2)}) copy-start(s32[64,64]{1,0:T(8,128)} %mask_ref.1) | copy-start | bytes 49156
  3.7 0.7 %copy-start.4 = (f32[512]{0:T(512)S(1)}, f32[512]{0:T(512)}, u32[]{:S(2)}) copy-start(f32[512]{0:T(512)} %param.11) | copy-start | bytes 6148

commit v2 on v1

--- a/solution.py
+++ b/solution.py
@@ -102,58 +102,10 @@
     rows = lik[...] * share
     lik[...] = rows / jnp.max(rows, axis=1, keepdims=True)
 
-    own = lax.broadcasted_iota(jnp.int32, (half, states), 0) + core * half
-    diagonal = own == lax.broadcasted_iota(jnp.int32, (half, states), 1)
-    start = pl.multiple_of(core * half, half)
-    part[...] = (moves[pl.ds(start, half), :] + jnp.where(diagonal, stay, 0.0)) * lik[0:1, :]
-    logs[...] = jnp.zeros_like(logs)
-    size = half // CHUNKS
-
-    def advance(t, rescale):
-        emitted = lik[pl.ds(t, 1), :]
-        for h in range(CHUNKS):
-            at = slice(h * size, (h + 1) * size)
-            a = part[at, :]
-            high, low = split(a)
-            high, low = high.astype(BF16), low.astype(BF16)
-            both = jnp.dot(
-                jnp.concatenate([high, low], axis=0), fwd_w[:, :states],
-                preferred_element_type=F32,
-            )
-            rest = jnp.dot(high, fwd_w[:, states:], preferred_element_type=F32)
-            new = (a * stay + (both[:size] + (both[size:] + rest))) * emitted
-            if rescale:
-                peak = jnp.max(a, axis=1, keepdims=True)
-                new = new * (1.0 / peak)
-                logs[at, :] = logs[at, :] + jnp.log(peak)
-            part[at, :] = new
-
-    def two(i, carry):
-        advance(1 + 2 * i, True)
-        advance(2 + 2 * i, False)
-        return carry
-
-    lax.fori_loop(0, (steps - 1) // 2, two, 0)
-    if (steps - 1) % 2:
-        advance(steps - 1, True)
-
-    final_log = logs[...]
-    own_peak = jnp.max(final_log + jnp.log(jnp.max(part[...], axis=1, keepdims=True)))
-    peak_out[...] = jnp.full(peak_out.shape, own_peak, F32)
     neighbours = 1 + 2 * (
         jnp.where(first, 0, 1).astype(jnp.int32) + jnp.where(last, 0, 1).astype(jnp.int32)
     )
     pl.semaphore_wait(barrier, neighbours)
-    peak_copy = pltpu.make_async_remote_copy(
-        src_ref=peak_out, dst_ref=peak_in, send_sem=peak_sems.at[0], recv_sem=peak_sems.at[1],
-        device_id={"state": 1 - core}, device_id_type=MESH,
-    )
-    peak_copy.start()
-    peak_copy.wait()
-    top = jnp.maximum(peak_out[0:1, 0:1], peak_in[0:1, 0:1])
-    whole = part[...] * jnp.exp(final_log - top)
-    put_pieces(chain_f, whole)
-    put_pieces(chain_b, jnp.transpose(whole))
 
     def fwd_copy(c):
         return pltpu.make_async_remote_copy(
@@ -183,15 +135,100 @@
             device_id={"state": 1 - core}, device_id_type=MESH,
         )
 
+    def ahead(i, a):
+        scale = 1.0 / jnp.max(a, axis=1, keepdims=True)
+        a = (a * stay + times(a, fwd_w[...])) * (lik[pl.ds(i, 1), :] * scale)
+        alphas[pl.ds(i, 1), :] = a
+        return a
+
+    def back(i, b):
+        t = steps - 1 - i
+        betas[pl.ds(t, 1), :] = b
+        x = b * lik[pl.ds(t, 1), :]
+        scale = 1.0 / jnp.max(x, axis=1, keepdims=True)
+        return (x * stay + times(x, bwd_w[...])) * scale
+
+    def opening():
+        a = fwd_in[0] + fwd_in[1]
+        return a / jnp.max(a, axis=1, keepdims=True)
+
+    def closing():
+        b = jnp.concatenate([bwd_in[0], bwd_in[1]], axis=1)
+        return b / jnp.max(b, axis=1, keepdims=True)
+
+    def walk_ahead():
+        return lax.fori_loop(0, steps, ahead, opening())
+
+    def walk_back():
+        return lax.fori_loop(0, steps, back, closing())
+
     @pl.when(first)
     def _():
         fwd_in[0] = jnp.exp(prior_ref[...])
         fwd_in[1] = jnp.zeros((1, states), F32)
+        fwd_out[...] = walk_ahead()
+        for c in range(2):
+            fwd_copy(c).start()
 
     @pl.when(last)
     def _():
         bwd_in[0] = jnp.ones((1, half), F32)
         bwd_in[1] = jnp.ones((1, half), F32)
+        b = walk_back()
+        bwd_out[...] = jnp.where(core == 0, b[:, :half], b[:, half:])
+        for c in range(2):
+            bwd_copy(c).start()
+
+    @pl.when(jnp.logical_not(jnp.logical_or(first, last)))
+    def _():
+        own = lax.broadcasted_iota(jnp.int32, (half, states), 0) + core * half
+        diagonal = own == lax.broadcasted_iota(jnp.int32, (half, states), 1)
+        start = pl.multiple_of(core * half, half)
+        part[...] = (moves[pl.ds(start, half), :] + jnp.where(diagonal, stay, 0.0)) * lik[0:1, :]
+        logs[...] = jnp.zeros_like(logs)
+        size = half // CHUNKS
+
+        def advance(t, rescale):
+            emitted = lik[pl.ds(t, 1), :]
+            for h in range(CHUNKS):
+                at = slice(h * size, (h + 1) * size)
+                a = part[at, :]
+                high, low = split(a)
+                high, low = high.astype(BF16), low.astype(BF16)
+                both = jnp.dot(
+                    jnp.concatenate([high, low], axis=0), fwd_w[:, :states],
+                    preferred_element_type=F32,
+                )
+                rest = jnp.dot(high, fwd_w[:, states:], preferred_element_type=F32)
+                new = (a * stay + (both[:size] + (both[size:] + rest))) * emitted
+                if rescale:
+                    peak = jnp.max(a, axis=1, keepdims=True)
+                    new = new * (1.0 / peak)
+                    logs[at, :] = logs[at, :] + jnp.log(peak)
+                part[at, :] = new
+
+        def two(i, carry):
+            advance(1 + 2 * i, True)
+            advance(2 + 2 * i, False)
+            return carry
+
+        lax.fori_loop(0, (steps - 1) // 2, two, 0)
+        if (steps - 1) % 2:
+            advance(steps - 1, True)
+
+        final_log = logs[...]
+        own_peak = jnp.max(final_log + jnp.log(jnp.max(part[...], axis=1, keepdims=True)))
+        peak_out[...] = jnp.full(peak_out.shape, own_peak, F32)
+        peak_copy = pltpu.make_async_remote_copy(
+            src_ref=peak_out, dst_ref=peak_in, send_sem=peak_sems.at[0], recv_sem=peak_sems.at[1],
+            device_id={"state": 1 - core}, device_id_type=MESH,
+        )
+        peak_copy.start()
+        peak_copy.wait()
+        top = jnp.maximum(peak_out[0:1, 0:1], peak_in[0:1, 0:1])
+        whole = part[...] * jnp.exp(final_log - top)
+        put_pieces(chain_f, whole)
+        put_pieces(chain_b, jnp.transpose(whole))
 
     def forward():
         @pl.when(jnp.logical_not(first))
@@ -223,36 +260,48 @@
                 bwd_copy(c).start()
 
     early = shard < shard_count // 2
+    gap = jnp.where(early, shard_count - 1 - 2 * shard, 2 * shard - shard_count + 1)
+    apart = jnp.logical_or(gap >= 3, jnp.logical_or(first, last))
 
     @pl.when(early)
     def _():
+        @pl.when(jnp.logical_not(first))
+        def _():
+            forward()
+
+            @pl.when(apart)
+            def _():
+                walk_ahead()
+
+        backward()
+
+        @pl.when(apart)
+        def _():
+            walk_back()
+
+    @pl.when(jnp.logical_not(early))
+    def _():
+        @pl.when(jnp.logical_not(last))
+        def _():
+            backward()
+
+            @pl.when(apart)
+            def _():
+                walk_back()
+
         forward()
-        backward()
-
-    @pl.when(jnp.logical_not(early))
-    def _():
-        backward()
-        forward()
-
-    a = fwd_in[0] + fwd_in[1]
-    a = a / jnp.max(a, axis=1, keepdims=True)
-    b = jnp.concatenate([bwd_in[0], bwd_in[1]], axis=1)
-    b = b / jnp.max(b, axis=1, keepdims=True)
-
-    def walk(i, carry):
-        a, b = carry
-        emitted = lik[pl.ds(i, 1), :]
-        scale = 1.0 / jnp.max(a, axis=1, keepdims=True)
-        a_new = (a * stay + times(a, fwd_w[...])) * (emitted * scale)
-        alphas[pl.ds(i, 1), :] = a_new
-        t = steps - 1 - i
-        betas[pl.ds(t, 1), :] = b
-        x = b * lik[pl.ds(t, 1), :]
-        scale = 1.0 / jnp.max(x, axis=1, keepdims=True)
-        b_new = (x * stay + times(x, bwd_w[...])) * scale
-        return a_new, b_new
-
-    lax.fori_loop(0, steps, walk, (a, b))
+
+        @pl.when(apart)
+        def _():
+            walk_ahead()
+
+    @pl.when(jnp.logical_not(apart))
+    def _():
+        def both(i, carry):
+            return ahead(i, carry[0]), back(i, carry[1])
+
+        lax.fori_loop(0, steps, both, (opening(), closing()))
+
     joint = alphas[...] * betas[...]
     factor = states / jnp.sum(joint, axis=1, keepdims=True)
     out_ref[...] = jnp.where(core == 0, joint[:, :half], joint[:, half:]) * factor

time: 61.1 us -> 53.9 us (0.88)
  Pallas kernels: 55.8 us -> 48.6 us
    pallas_call x1, Pallas kernels: 55.8 us -> 48.6 us  [shards(): pl.pallas_call(functools.partial(kernel, shard_count), out_shape=jax.Shap...]
where the time goes in v2:
time: 53.9 us; the launch traced here: 53.6 us
  Pallas kernels  48.6 us (90%)
  local copies, waits for them, and re-layouts  5 us (9%)
    pallas_call x1, Pallas kernels, shards(): pl.pallas_call(functools.partial(kernel, shard_count), out_shape=jax.Shap...  48.6 us
    unnamed x13, local copies, waits for them, and re-layouts  5 us

profile of v2, /device:TPU:0, one launch (start us, length us, event | category | flops | bytes accessed | tf_op | source)
XLA Modules:
  0.0 53.6 jit_solution(11604153108472760452)
XLA Ops:
  0.0 0.0 copy-start.3
  0.0 0.0 copy-start.5
  0.0 0.7 %copy-done.3 = f32[512]{0:T(512)S(1)} copy-done((f32[512]{0:T(512)S(1)}, f32[512]{0:T(512)}, u32[]{:S(2)}) %copy-start.3) | copy-done | bytes 2072
  0.7 0.0 copy-done.5
  0.7 0.0 copy-start
  0.7 1.2 %copy-done = f32[512,512]{1,0:T(8,128)S(1)} copy-done((f32[512,512]{1,0:T(8,128)S(1)}, f32[512,512]{1,0:T(8,128)}, u32[]{:S(2)}) %copy-start) | copy-done | bytes 1048600
  1.9 0.0 copy-start.1
  1.9 1.0 %copy-done.1 = f32[256,512]{1,0:T(8,128)S(1)} copy-done((f32[256,512]{1,0:T(8,128)S(1)}, f32[256,512]{1,0:T(8,128)}, u32[]{:S(2)}) %copy-start.1) | copy-done | bytes 524312
  3.0 0.0 copy-start.2
  3.0 0.8 %copy-done.2 = s32[64,64]{1,0:T(8,128)S(1)} copy-done((s32[64,64]{1,0:T(8,128)S(1)}, s32[64,64]{1,0:T(8,128)}, u32[]{:S(2)}) %copy-start.2) | copy-done | bytes 16408
  3.7 0.0 copy-start.4
  3.7 0.7 %copy-done.4 = f32[512]{0:T(512)S(1)} copy-done((f32[512]{0:T(512)S(1)}, f32[512]{0:T(512)}, u32[]{:S(2)}) %copy-start.4) | copy-done | bytes 2072
  4.4 48.6 %shard_map.64 = f32[32,256]{1,0:T(8,128)S(1)} custom-call(s32[32]{0:T(128)S(1)} %copy-done.5, s32[64,64]{1,0:T(8,128)S(1)} %copy-done.2, f32[512,512]{1,0:T(8,128)S(1)} %copy-done, f32[1,512]{1,0:T(1,128)S(1)} %bitcast.2, f32[256,512]{1,0:T(8,128)S(1)} %copy-done.1, f32[1,512]{1,0:T(1,128)S(1)} %bitcast.3), custom_call_target="tpu_custom_call" | custom-call | tf_op jit(solution)/shard_map/pallas_call | solution.py:326
  53.0 0.6 %copy.8 = f32[32,256]{1,0:T(8,128)} copy(f32[32,256]{1,0:T(8,128)S(1)} %shard_map.64) | data formatting | bytes 65536
Async XLA Ops:
  0.0 0.7 %copy-start.3 = (f32[512]{0:T(512)S(1)}, f32[512]{0:T(512)}, u32[]{:S(2)}) copy-start(f32[512]{0:T(512)} %param.9) | copy-start | bytes 6148
  0.0 0.7 %copy-start.5 = (s32[32]{0:T(128)S(1)}, s32[32]{0:T(128)}, u32[]{:S(2)}) copy-start(s32[32]{0:T(128)} %observed_ref.1) | copy-start | bytes 388
  0.7 1.2 %copy-start = (f32[512,512]{1,0:T(8,128)S(1)}, f32[512,512]{1,0:T(8,128)}, u32[]{:S(2)}) copy-start(f32[512,512]{1,0:T(8,128)} %jump_ref.1) | copy-start | bytes 3145732
  1.9 1.0 %copy-start.1 = (f32[256,512]{1,0:T(8,128)S(1)}, f32[256,512]{1,0:T(8,128)}, u32[]{:S(2)}) copy-start(f32[256,512]{1,0:T(8,128)} %emit_ref.1) | copy-start | bytes 1572868
  3.0 0.8 %copy-start.2 = (s32[64,64]{1,0:T(8,128)S(1)}, s32[64,64]{1,0:T(8,128)}, u32[]{:S(2)}) copy-start(s32[64,64]{1,0:T(8,128)} %mask_ref.1) | copy-start | bytes 49156
  3.7 0.7 %copy-start.4 = (f32[512]{0:T(512)S(1)}, f32[512]{0:T(512)}, u32[]{:S(2)}) copy-start(f32[512]{0:T(512)} %param.11) | copy-start | bytes 6148

commit v3 on v2

--- a/solution.py
+++ b/solution.py
@@ -157,10 +157,10 @@
         return b / jnp.max(b, axis=1, keepdims=True)
 
     def walk_ahead():
-        return lax.fori_loop(0, steps, ahead, opening())
+        return lax.fori_loop(0, steps, ahead, opening(), unroll=4)
 
     def walk_back():
-        return lax.fori_loop(0, steps, back, closing())
+        return lax.fori_loop(0, steps, back, closing(), unroll=4)
 
     @pl.when(first)
     def _():

time: 53.9 us -> 53.2 us (0.987)
  Pallas kernels: 48.6 us -> 47.9 us
    pallas_call x1, Pallas kernels: 48.6 us -> 47.9 us  [shards(): pl.pallas_call(functools.partial(kernel, shard_count), out_shape=jax.Shap...]
where the time goes in v3:
time: 53.2 us; the launch traced here: 52.9 us
  Pallas kernels  47.9 us (90%)
  local copies, waits for them, and re-layouts  5 us (9%)
    pallas_call x1, Pallas kernels, shards(): pl.pallas_call(functools.partial(kernel, shard_count), out_shape=jax.Shap...  47.9 us
    unnamed x13, local copies, waits for them, and re-layouts  5 us

profile of v3, /device:TPU:0, one launch (start us, length us, event | category | flops | bytes accessed | tf_op | source)
XLA Modules:
  0.0 52.9 jit_solution(13151705068386142341)
XLA Ops:
  0.0 0.0 copy-start.3
  0.0 0.0 copy-start.5
  0.0 0.7 %copy-done.3 = f32[512]{0:T(512)S(1)} copy-done((f32[512]{0:T(512)S(1)}, f32[512]{0:T(512)}, u32[]{:S(2)}) %copy-start.3) | copy-done | bytes 2072
  0.7 0.0 copy-done.5
  0.7 0.0 copy-start
  0.7 1.2 %copy-done = f32[512,512]{1,0:T(8,128)S(1)} copy-done((f32[512,512]{1,0:T(8,128)S(1)}, f32[512,512]{1,0:T(8,128)}, u32[]{:S(2)}) %copy-start) | copy-done | bytes 1048600
  1.9 0.0 copy-start.1
  1.9 1.0 %copy-done.1 = f32[256,512]{1,0:T(8,128)S(1)} copy-done((f32[256,512]{1,0:T(8,128)S(1)}, f32[256,512]{1,0:T(8,128)}, u32[]{:S(2)}) %copy-start.1) | copy-done | bytes 524312
  3.0 0.0 copy-start.2
  3.0 0.8 %copy-done.2 = s32[64,64]{1,0:T(8,128)S(1)} copy-done((s32[64,64]{1,0:T(8,128)S(1)}, s32[64,64]{1,0:T(8,128)}, u32[]{:S(2)}) %copy-start.2) | copy-done | bytes 16408
  3.7 0.0 copy-start.4
  3.7 0.7 %copy-done.4 = f32[512]{0:T(512)S(1)} copy-done((f32[512]{0:T(512)S(1)}, f32[512]{0:T(512)}, u32[]{:S(2)}) %copy-start.4) | copy-done | bytes 2072
  4.4 47.9 %shard_map.64 = f32[32,256]{1,0:T(8,128)S(1)} custom-call(s32[32]{0:T(128)S(1)} %copy-done.5, s32[64,64]{1,0:T(8,128)S(1)} %copy-done.2, f32[512,512]{1,0:T(8,128)S(1)} %copy-done, f32[1,512]{1,0:T(1,128)S(1)} %bitcast.2, f32[256,512]{1,0:T(8,128)S(1)} %copy-done.1, f32[1,512]{1,0:T(1,128)S(1)} %bitcast.3), custom_call_target="tpu_custom_call" | custom-call | tf_op jit(solution)/shard_map/pallas_call | solution.py:326
  52.3 0.6 %copy.8 = f32[32,256]{1,0:T(8,128)} copy(f32[32,256]{1,0:T(8,128)S(1)} %shard_map.64) | data formatting | bytes 65536
Async XLA Ops:
  0.0 0.7 %copy-start.3 = (f32[512]{0:T(512)S(1)}, f32[512]{0:T(512)}, u32[]{:S(2)}) copy-start(f32[512]{0:T(512)} %param.9) | copy-start | bytes 6148
  0.0 0.7 %copy-start.5 = (s32[32]{0:T(128)S(1)}, s32[32]{0:T(128)}, u32[]{:S(2)}) copy-start(s32[32]{0:T(128)} %observed_ref.1) | copy-start | bytes 388
  0.7 1.2 %copy-start = (f32[512,512]{1,0:T(8,128)S(1)}, f32[512,512]{1,0:T(8,128)}, u32[]{:S(2)}) copy-start(f32[512,512]{1,0:T(8,128)} %jump_ref.1) | copy-start | bytes 3145732
  1.9 1.0 %copy-start.1 = (f32[256,512]{1,0:T(8,128)S(1)}, f32[256,512]{1,0:T(8,128)}, u32[]{:S(2)}) copy-start(f32[256,512]{1,0:T(8,128)} %emit_ref.1) | copy-start | bytes 1572868
  3.0 0.8 %copy-start.2 = (s32[64,64]{1,0:T(8,128)S(1)}, s32[64,64]{1,0:T(8,128)}, u32[]{:S(2)}) copy-start(s32[64,64]{1,0:T(8,128)} %mask_ref.1) | copy-start | bytes 49156
  3.7 0.7 %copy-start.4 = (f32[512]{0:T(512)S(1)}, f32[512]{0:T(512)}, u32[]{:S(2)}) copy-start(f32[512]{0:T(512)} %param.11) | copy-start | bytes 6148

commit v4 on v3

--- a/solution.py
+++ b/solution.py
@@ -212,7 +212,7 @@
             advance(2 + 2 * i, False)
             return carry
 
-        lax.fori_loop(0, (steps - 1) // 2, two, 0)
+        lax.fori_loop(0, (steps - 1) // 2, two, 0, unroll=3)
         if (steps - 1) % 2:
             advance(steps - 1, True)
 

time: 53.2 us -> 51.6 us (0.970)
  Pallas kernels: 47.9 us -> 46.3 us
    pallas_call x1, Pallas kernels: 47.9 us -> 46.3 us  [shards(): pl.pallas_call(functools.partial(kernel, shard_count), out_shape=jax.Shap...]
where the time goes in v4:
time: 51.6 us; the launch traced here: 51.3 us
  Pallas kernels  46.3 us (90%)
  local copies, waits for them, and re-layouts  5 us (10%)
    pallas_call x1, Pallas kernels, shards(): pl.pallas_call(functools.partial(kernel, shard_count), out_shape=jax.Shap...  46.3 us
    unnamed x13, local copies, waits for them, and re-layouts  5 us

profile of v4, /device:TPU:0, one launch (start us, length us, event | category | flops | bytes accessed | tf_op | source)
XLA Modules:
  0.0 51.3 jit_solution(10211763725571090608)
XLA Ops:
  0.0 0.0 copy-start.3
  0.0 0.0 copy-start.5
  0.0 0.7 %copy-done.3 = f32[512]{0:T(512)S(1)} copy-done((f32[512]{0:T(512)S(1)}, f32[512]{0:T(512)}, u32[]{:S(2)}) %copy-start.3) | copy-done | bytes 2072
  0.7 0.0 copy-done.5
  0.7 0.0 copy-start
  0.7 1.2 %copy-done = f32[512,512]{1,0:T(8,128)S(1)} copy-done((f32[512,512]{1,0:T(8,128)S(1)}, f32[512,512]{1,0:T(8,128)}, u32[]{:S(2)}) %copy-start) | copy-done | bytes 1048600
  1.9 0.0 copy-start.1
  1.9 1.0 %copy-done.1 = f32[256,512]{1,0:T(8,128)S(1)} copy-done((f32[256,512]{1,0:T(8,128)S(1)}, f32[256,512]{1,0:T(8,128)}, u32[]{:S(2)}) %copy-start.1) | copy-done | bytes 524312
  3.0 0.0 copy-start.2
  3.0 0.8 %copy-done.2 = s32[64,64]{1,0:T(8,128)S(1)} copy-done((s32[64,64]{1,0:T(8,128)S(1)}, s32[64,64]{1,0:T(8,128)}, u32[]{:S(2)}) %copy-start.2) | copy-done | bytes 16408
  3.7 0.0 copy-start.4
  3.7 0.7 %copy-done.4 = f32[512]{0:T(512)S(1)} copy-done((f32[512]{0:T(512)S(1)}, f32[512]{0:T(512)}, u32[]{:S(2)}) %copy-start.4) | copy-done | bytes 2072
  4.4 46.3 %shard_map.64 = f32[32,256]{1,0:T(8,128)S(1)} custom-call(s32[32]{0:T(128)S(1)} %copy-done.5, s32[64,64]{1,0:T(8,128)S(1)} %copy-done.2, f32[512,512]{1,0:T(8,128)S(1)} %copy-done, f32[1,512]{1,0:T(1,128)S(1)} %bitcast.2, f32[256,512]{1,0:T(8,128)S(1)} %copy-done.1, f32[1,512]{1,0:T(1,128)S(1)} %bitcast.3), custom_call_target="tpu_custom_call" | custom-call | tf_op jit(solution)/shard_map/pallas_call | solution.py:326
  50.7 0.6 %copy.8 = f32[32,256]{1,0:T(8,128)} copy(f32[32,256]{1,0:T(8,128)S(1)} %shard_map.64) | data formatting | bytes 65536
Async XLA Ops:
  0.0 0.7 %copy-start.3 = (f32[512]{0:T(512)S(1)}, f32[512]{0:T(512)}, u32[]{:S(2)}) copy-start(f32[512]{0:T(512)} %param.9) | copy-start | bytes 6148
  0.0 0.7 %copy-start.5 = (s32[32]{0:T(128)S(1)}, s32[32]{0:T(128)}, u32[]{:S(2)}) copy-start(s32[32]{0:T(128)} %observed_ref.1) | copy-start | bytes 388
  0.7 1.2 %copy-start = (f32[512,512]{1,0:T(8,128)S(1)}, f32[512,512]{1,0:T(8,128)}, u32[]{:S(2)}) copy-start(f32[512,512]{1,0:T(8,128)} %jump_ref.1) | copy-start | bytes 3145732
  1.9 1.0 %copy-start.1 = (f32[256,512]{1,0:T(8,128)S(1)}, f32[256,512]{1,0:T(8,128)}, u32[]{:S(2)}) copy-start(f32[256,512]{1,0:T(8,128)} %emit_ref.1) | copy-start | bytes 1572868
  3.0 0.8 %copy-start.2 = (s32[64,64]{1,0:T(8,128)S(1)}, s32[64,64]{1,0:T(8,128)}, u32[]{:S(2)}) copy-start(s32[64,64]{1,0:T(8,128)} %mask_ref.1) | copy-start | bytes 49156
  3.7 0.7 %copy-start.4 = (f32[512]{0:T(512)S(1)}, f32[512]{0:T(512)}, u32[]{:S(2)}) copy-start(f32[512]{0:T(512)} %param.11) | copy-start | bytes 6148
